TPU v7x, 256 devices: a whole 4x4x8 slice. The times are simulated.
256 devices in a mesh: section: 4 (over y_lo, core), dp: 8 (over z), expert: 8 (over x, y_hi).
Axes of the slice: x: 4, y: 4 (y_hi: 2, y_lo: 2; y = y_hi * 2 + y_lo), z: 8, core: 2. Of those that a mesh axis runs over, the one named last changes fastest.
Arguments:
- grad_out: bfloat16 [4, 8192, 3072], P('section', ('dp', 'expert')), may hold values from -6 to 6
- expert_ids: int32 [4, 8192, 2], P('section', ('dp', 'expert')), may hold values from 0 to 7, as said below
- slot_ids: int32 [4, 8192, 2], P('section', ('dp', 'expert')), may hold values from 0 to 35, as said below
- gates: float32 [4, 8192, 2], P('section', ('dp', 'expert')), may hold values from 0.1 to 1
- hidden: bfloat16 [4, 2304, 32768], P('section', None, ('dp', 'expert')), may hold values from -0.3984375 to 0.3984375
- w_down: bfloat16 [4, 32768, 3072], P('section', ('dp', 'expert')), may hold values from -0.0625 to 0.0625
Outputs:
- hidden_grad: bfloat16 [4, 2304, 32768], P('section', None, ('dp', 'expert'))
- weight_grad: bfloat16 [4, 32768, 3072], P('section', ('dp', 'expert'))
Inputs may be any that keep to these rules, and one draw needn't show every extreme that they name: `expert_ids`: each token names 2 different experts. Within one block of 128 rows at most 36 routes go to one expert, and in every section one expert below 4 receives exactly 36 routes from each of its 64 blocks. `slot_ids`: the routes of one block to one expert take the slots 0 to their count minus one, each once.
All inputs are finite; a program needn't handle non-finite values.
Results may differ from a plain program's by a relative error of at most 0.0049.
Values may be sent and summed in bfloat16 or wider, within the bound.
A program may use at most 128 MiB of HBM per device.

v0:
```python
import jax
import jax.numpy as jnp
from jax import lax
from jax.sharding import PartitionSpec as P

FLIGHT = 4


def passed_along(block, axis, distance):
    devices = range(lax.axis_size(axis))
    route = [(i - distance, i) for i in devices if i - distance in devices]
    return lax.ppermute(block, axis, route)


def body(grad_out, expert_ids, slot_ids, gates, hidden, w_down):
    tok_rows = grad_out.shape[1]
    features = grad_out.shape[2]
    selected_expert_count = expert_ids.shape[2]
    dp_count = lax.axis_size("dp")
    expert_count = lax.axis_size("expert")
    sources = dp_count * expert_count
    total_slot_count = hidden.shape[1]
    capacity = total_slot_count // sources
    holders = sources // FLIGHT
    scaled = (gates[0][..., None] * grad_out[0][:, None, :].astype(jnp.float32)).astype(
        jnp.bfloat16
    )
    routes = scaled.reshape(tok_rows * selected_expert_count, features)
    slot_index = (expert_ids[0] * capacity + slot_ids[0]).reshape(-1)
    indicator_matrix = (
        slot_index[:, None] == jnp.arange(FLIGHT * capacity, dtype=jnp.int32)[None, :]
    ).astype(jnp.bfloat16)
    compact = lax.dot_general(
        indicator_matrix, routes, (((0,), (0,)), ((), ())), preferred_element_type=jnp.float32
    )
    compact = compact.astype(jnp.bfloat16).reshape(FLIGHT, capacity, features)
    outgoing = jnp.repeat(compact, holders, axis=0)
    weight = w_down[0]
    own_hidden = hidden[0]
    arrived = lax.all_to_all(
        outgoing, ("dp", "expert"), split_axis=0, concat_axis=0, tiled=True
    ).reshape(total_slot_count, features)
    section_part = lax.dot_general(
        arrived, weight, (((1,), (1,)), ((), ())), preferred_element_type=jnp.float32
    ).astype(jnp.bfloat16)
    weight_part = lax.dot_general(
        own_hidden, arrived, (((0,), (0,)), ((), ())), preferred_element_type=jnp.float32
    ).astype(jnp.bfloat16)
    incoming = passed_along(section_part, "section", -1)
    return (incoming[None], weight_part[None])


def solution(mesh):
    in_specs = (
        P("section", ("dp", "expert"), None),
        P("section", ("dp", "expert"), None),
        P("section", ("dp", "expert"), None),
        P("section", ("dp", "expert"), None),
        P("section", None, ("dp", "expert")),
        P("section", ("dp", "expert"), None),
    )
    out_specs = (P("section", None, ("dp", "expert")), P("section", ("dp", "expert"), None))
    return jax.shard_map(body, mesh=mesh, in_specs=in_specs, out_specs=out_specs, check_vma=False)
```

profile of v0, /device:TPU:1, one launch (start us, length us, event | category | flops | bytes accessed | tf_op | source)
XLA Modules:
  0.0 445.3 jit_solution(14725824494792357192)
XLA Ops:
  0.6 0.0 copy-start
  0.6 0.8 multiply_add_fusion
  1.5 0.1 copy.9
  1.6 0.1 add.11
  1.8 0.8 copy.10
  2.5 0.1 mul.31
  2.7 1.3 bitcast_convert_fusion
  4.0 2.7 mul.33
  6.7 5.2 %mul.34 = f32[256,3072]{1,0:T(8,128)} reshape(f32[128,2,3072]{2,1,0:T(2,128)} %mul.33) | data formatting | bytes 6291456 | tf_op jit(solution)/shard_map/mul | solution.py:25
  12.0 3.3 convolution_convert_fusion.2
  15.3 2.3 reshape.40
  17.6 3.8 broadcast_in_dim.10
  21.4 356.8 %all_to_all.5 = bf16[64,36,3072]{2,1,0:T(8,128)(2,1)} all-to-all(bf16[64,36,3072]{2,1,0:T(8,128)(2,1)S(1)} %bitcast.17), channel_id=1, replica_groups=mesh['section'=4,'dp'=8,'expert'=8] {'dp','expert'}, dimensions={0} | all-to-all | bytes 28311552 | tf_op jit(solution)/shard_map/all_to_all | solution.py:40
  378.2 17.0 %reshape.42 = bf16[2304,3072]{1,0:T(8,128)(2,1)} reshape(bf16[64,36,3072]{2,1,0:T(8,128)(2,1)} %all_to_all.5) | data formatting | bytes 28311552 | tf_op jit(solution)/shard_map/reshape | solution.py:42
  395.2 0.0 copy-done
  395.2 13.5 %convolution_convert_fusion.1 = bf16[2304,512]{1,0:T(8,128)(2,1)} fusion(bf16[2304,3072]{1,0:T(8,128)(2,1)} %reshape.42, bf16[1,512,3072]{2,1,0:T(8,128)(2,1)S(1)} %copy-done), kind=kOutput, calls=%fused_computation.1 | convolution fusion | flops 7248936960 | bytes 19660800 | tf_op jit(solution)/shard_map/dot_general | solution.py:43
  408.7 6.4 %collective-permute-start = (bf16[2304,512]{1,0:T(8,128)(2,1)}, bf16[2304,512]{1,0:T(8,128)(2,1)}, u32[]{:S(2)}, u32[]{:S(2)}) collective-permute-start(bf16[2304,512]{1,0:T(8,128)(2,1)} %convolution_convert_fusion.1), channel_id=1, source_target_pairs={{64,0},{128,64},{192,128},{65,1},{129,65},{193,129},{66,2},{130,66... | collective-permute-start | bytes 7077896 | tf_op jit(solution)/shard_map/ppermute | solution.py:12
  415.1 0.0 copy-done.2
  415.1 0.0 copy-done.3
  415.1 9.1 %fusion = bf16[1,512,3072]{1,2,0:T(8,128)(2,1)} fusion(bf16[2304,3072]{1,0:T(8,128)(2,1)S(1)} %copy-done.2, bf16[1,2304,512]{2,1,0:T(8,128)(2,1)S(1)} %copy-done.3), kind=kOutput, calls=%fused_computation.2 | convolution fusion | flops 7249330176 | bytes 19660800 | tf_op jit(solution)/shard_map/dot_general | solution.py:46
  424.2 4.8 %copy.11 = bf16[1,512,3072]{2,1,0:T(8,128)(2,1)} copy(bf16[1,512,3072]{1,2,0:T(8,128)(2,1)} %fusion) | data formatting | bytes 6291456
  429.0 13.1 %collective-permute-done = bf16[2304,512]{1,0:T(8,128)(2,1)} collective-permute-done((bf16[2304,512]{1,0:T(8,128)(2,1)}, bf16[2304,512]{1,0:T(8,128)(2,1)}, u32[]{:S(2)}, u32[]{:S(2)}) %collective-permute-start) | collective-permute-done | bytes 2359328 | tf_op jit(solution)/shard_map/ppermute | solution.py:12
  442.0 3.2 copy.13
  445.3 0.0 copy-done.1
  (3 shorter events, 0.0 us)
Async XLA Ops:
  0.6 394.6 %copy-start = (bf16[1,512,3072]{2,1,0:T(8,128)(2,1)S(1)}, bf16[1,512,3072]{2,1,0:T(8,128)(2,1)}, u32[]{:S(2)}) copy-start(bf16[1,512,3072]{2,1,0:T(8,128)(2,1)} %param.11) | copy-start | bytes 9437188
  395.2 19.9 %copy-start.2 = (bf16[2304,3072]{1,0:T(8,128)(2,1)S(1)}, bf16[2304,3072]{1,0:T(8,128)(2,1)}, u32[]{:S(2)}) copy-start(bf16[2304,3072]{1,0:T(8,128)(2,1)} %reshape.42) | copy-start | bytes 42467332
  395.2 19.9 %copy-start.3 = (bf16[1,2304,512]{2,1,0:T(8,128)(2,1)S(1)}, bf16[1,2304,512]{2,1,0:T(8,128)(2,1)}, u32[]{:S(2)}) copy-start(bf16[1,2304,512]{2,1,0:T(8,128)(2,1)} %param.10) | copy-start | bytes 7077892
  408.7 33.3 %collective-permute-start = (bf16[2304,512]{1,0:T(8,128)(2,1)}, bf16[2304,512]{1,0:T(8,128)(2,1)}, u32[]{:S(2)}, u32[]{:S(2)}) collective-permute-start(bf16[2304,512]{1,0:T(8,128)(2,1)} %convolution_convert_fusion.1), channel_id=1, source_target_pairs={{64,0},{128,64},{192,128},{65,1},{129,65},{193,129},{66,2},{130,66... | collective-permute-start | bytes 7077896 | tf_op jit(solution)/shard_map/ppermute | solution.py:12
  424.2 21.1 %copy-start.1 = (bf16[1,512,3072]{2,1,0:T(8,128)(2,1)S(1)}, bf16[1,512,3072]{2,1,0:T(8,128)(2,1)}, u32[]{:S(2)}) copy-start(bf16[1,512,3072]{2,1,0:T(8,128)(2,1)} %param.11) | copy-start | bytes 9437188
where the time goes:
time: 446 us; the launch traced here: 445 us
  blocking collectives  357 us (80%)
  local copies, waits for them, and re-layouts  40.3 us (9%)
  matrix products  25.9 us (6%)
  waiting for transfers between devices  13.1 us (3%)
  starting transfers between devices  6.38 us (1%)
    all_to_all x1, blocking collectives, body(): lax.all_to_all(outgoing, ('dp', 'expert'), split_axis=0, concat_axis=0, t...  357 us
    reshape x1, local copies, waits for them, and re-layouts, body(): arrived = lax.all_to_all(outgoing, ('dp', 'expert'), split_axis=0, concat...  17 us
    dot_general x1, matrix products, body(): lax.dot_general(arrived, weight, (((1,), (1,)), ((), ())), preferred_elem...  13.5 us
    ppermute x1, waiting for transfers between devices, passed_along(): return lax.ppermute(block, axis, route)  13.1 us
    dot_general x1, matrix products, body(): lax.dot_general(own_hidden, arrived, (((0,), (0,)), ((), ())), preferred_...  9.05 us
  transfers between devices with their start and end apart: 1, of which 1 were waited for; matrix products, arithmetic and copies ran while one was open for 3% of the time, Pallas kernels for 0%

commit v1 on v0

v1 whole, which is shorter than its diff:
```python
import functools

import jax
import jax.numpy as jnp
from jax import lax
from jax.experimental import pallas as pl
from jax.experimental.pallas import tpu as pltpu
from jax.sharding import PartitionSpec as P

MESH = pl.DeviceIdType.MESH
FLIGHT = 4
BF16, F32, I32 = jnp.bfloat16, jnp.float32, jnp.int32

D = 3072
CAP = 36
BAND = 16
TAIL = CAP - 2 * BAND
QUARTER = D // 4
WIDTH = 2 * D + QUARTER
UNITS = 512
BLOCKS = 8
PLANE = 8
ROWS = PLANE * CAP
SLOTS = BLOCKS * ROWS
MAIN = PLANE * 2 * BAND
TAILS = PLANE * TAIL
HALF_A = 17 * 128
HALF_B = (WIDTH - 2 * HALF_A) // 2
A_ALL = (0, 2 * HALF_A)
A_0 = (0, HALF_A)
A_1 = (HALF_A, HALF_A)
B_ALL = (2 * HALF_A, 2 * HALF_B)
B_0 = (2 * HALF_A, HALF_B)
B_1 = (2 * HALF_A + HALF_B, HALF_B)
SEM_OF = {A_ALL: 0, A_0: 0, A_1: 1, B_ALL: 2, B_0: 2, B_1: 3}


def iota(shape, dim):
    return lax.broadcasted_iota(I32, shape, dim)


def onehot(cond):
    return cond.astype(F32).astype(BF16)


def dot(a, b, dims=((1,), (0,))):
    return lax.dot_general(a, b, (dims, ((), ())), preferred_element_type=F32)


def kernel(ids_ref, slots_ref, gates_ref, grad_hbm, hid_hbm, w_hbm, hout, wout,
           arr, outg, grad, hid, w, hmain, htail, utail, acc, sec, wbuf,
           in_sem, loc_sem, out_sem, send_sem, recv_sem, hsend_sem, hrecv_sem):
    section = lax.axis_index("section")
    z = lax.axis_index("dp")
    xy = lax.axis_index("expert")
    x, yh = lax.div(xy, 2), lax.rem(xy, 2)
    zb = lax.rem(z, 2)
    e = lax.div(z, 2)
    sg = 2 * zb - 1

    grad_in = pltpu.make_async_copy(grad_hbm, grad, in_sem.at[0])
    grad_in.start()
    hid_in = pltpu.make_async_copy(hid_hbm, hid, in_sem.at[1])
    hid_in.start()
    w_in = pltpu.make_async_copy(w_hbm, w, in_sem.at[2])
    w_in.start()

    def device(dz, dx, flip, ds=0):
        to_y = 1 - yh if flip else yh
        return (section + ds, lax.rem(z + dz + 8, 8), lax.rem(x + dx + 4, 4) * 2 + to_y)

    zflip = 1 - 2 * zb
    to_z = device(zflip, 0, False)
    to_y = device(0, 0, True)
    to_right = device(0, 1, False)
    to_left = device(0, -1, False)
    transit = {1: device(sg, 0, False), 2: device(-2 * sg, 0, False), 3: device(3 * sg, 0, False)}
    transit_from = {1: transit[1], 2: device(2 * sg, 0, False), 3: transit[3]}

    barrier = pltpu.get_barrier_semaphore()
    after = (lax.rem(section + 1, 4), z, xy)
    for other in (to_z, to_y, to_right, to_left, transit_from[1], transit_from[2], transit_from[3], after):
        pl.semaphore_signal(barrier, inc=1, device_id=other, device_id_type=MESH)

    def chunk_expert(j):
        return lax.rem(e + {0: 0, 1: sg, 2: -sg, 3: 2}[j] + 4, 4)

    experts = [chunk_expert(j) for j in range(4)]

    def expert_rows(j):
        base = jnp.full(j.shape, experts[3] * CAP, I32)
        for k in (2, 1, 0):
            base = jnp.where(j == k, experts[k] * CAP, base)
        return base

    place = ids_ref[...] * CAP + slots_ref[...]
    place0, place1 = place[0:1, :], place[1:2, :]
    gate0, gate1 = gates_ref[0:1, :], gates_ref[1:2, :]
    m = iota((128, 1), 0)
    want = expert_rows((m >> 4) & 3) + 16 * (m >> 6) + (m & 15)
    hit0, hit1 = place0 == want, place1 == want
    pick_main = onehot(hit0 | hit1)
    gate_main = jnp.sum(jnp.where(hit0, gate0, 0.0) + jnp.where(hit1, gate1, 0.0), axis=1, keepdims=True)
    m = iota((64, 1), 0)
    quarter = (m >> 2) & 3
    want = expert_rows(m >> 4) + 2 * BAND + (m & 3)
    hit0, hit1 = place0 == want, place1 == want
    tail_hit = hit0 | hit1
    gate_tail = jnp.sum(jnp.where(hit0, gate0, 0.0) + jnp.where(hit1, gate1, 0.0), axis=1, keepdims=True)

    def slot_of(j, dx=0, fy=False, fz=False):
        tz = z + zflip if fz else z
        tsg = -sg if fz else sg
        ty = 1 - yh if fy else yh
        return lax.rem(tz + tsg * j + 8, 8) * PLANE + lax.rem(x + dx + 4, 4) * 2 + ty

    mine = slot_of(0)
    grad_in.wait()
    for h in range(2):
        for c in range(0, D, 512):
            part = dot(pick_main[64 * h:64 * h + 64, :], grad[:, c:c + 512])
            part = (part * gate_main[64 * h:64 * h + 64, :]).astype(BF16)
            arr[mine, :, h * D + c:h * D + c + 512] = part[0:16]
            for j in (1, 2, 3):
                outg[j - 1, :, h * D + c:h * D + c + 512] = part[16 * j:16 * j + 16]
    part = jnp.zeros((64, QUARTER), F32)
    for q in range(4):
        part += dot(onehot(tail_hit & (quarter == q)), grad[:, q * QUARTER:(q + 1) * QUARTER])
    part = (part * gate_tail).astype(BF16)
    arr[mine, :, 2 * D:WIDTH] = part[0:16]
    for j in (1, 2, 3):
        outg[j - 1, :, 2 * D:WIDTH] = part[16 * j:16 * j + 16]

    pl.semaphore_wait(barrier, 8)

    sends = []

    def copy_of(slot, cols, to, n):
        piece = arr.at[slot, :, pl.ds(cols[0], cols[1])]
        return pltpu.make_async_remote_copy(
            src_ref=piece, dst_ref=piece, send_sem=send_sem.at[n],
            recv_sem=recv_sem.at[slot, SEM_OF[cols]], device_id=to, device_id_type=MESH)

    def send(slot, cols, to):
        copy = copy_of(slot, cols, to, len(sends))
        copy.start()
        sends.append(copy)

    def landed(slot, cols):
        copy_of(slot, cols, to_z, 0).wait_recv()

    def send_transit(j):
        copy = pltpu.make_async_remote_copy(
            src_ref=outg.at[j - 1], dst_ref=arr.at[mine], send_sem=send_sem.at[len(sends)],
            recv_sem=recv_sem.at[mine, 0], device_id=transit[j], device_id_type=MESH)
        copy.start()
        sends.append(copy)

    def wait_transit(j):
        slot = slot_of(j)
        pltpu.make_async_remote_copy(
            src_ref=outg.at[0], dst_ref=arr.at[slot], send_sem=send_sem.at[0],
            recv_sem=recv_sem.at[slot, 0], device_id=to_z, device_id_type=MESH).wait_recv()

    def stage0(j):
        if j:
            wait_transit(j)
        send(slot_of(j), A_ALL, to_z)
        send(slot_of(j), B_ALL, to_right)
        send(slot_of(j), B_ALL, to_left)

    def stage1(j):
        landed(slot_of(j, fz=True), A_ALL)
        send(slot_of(j), A_ALL, to_y)
        send(slot_of(j, fz=True), A_ALL, to_y)
        landed(slot_of(j, dx=-1), B_ALL)
        send(slot_of(j, dx=-1), B_0, to_right)
        landed(slot_of(j, dx=1), B_ALL)
        send(slot_of(j, dx=1), B_1, to_left)

    def stage2(j):
        for fy in (False, True):
            for fz in (False, True):
                if fy:
                    landed(slot_of(j, fy=True, fz=fz), A_ALL)
                send(slot_of(j, fy=fy, fz=fz), A_ALL, to_right)
                send(slot_of(j, fy=fy, fz=fz), A_ALL, to_left)
        for dx in (0, -1, 1):
            send(slot_of(j, dx=dx), B_ALL, to_y)
        landed(slot_of(j, dx=2), B_0)
        landed(slot_of(j, dx=2), B_1)
        send(slot_of(j, dx=2), B_ALL, to_y)

    def stage3(j):
        for fy in (False, True):
            for fz in (False, True):
                landed(slot_of(j, dx=-1, fy=fy, fz=fz), A_ALL)
                send(slot_of(j, dx=-1, fy=fy, fz=fz), A_0, to_right)
                landed(slot_of(j, dx=1, fy=fy, fz=fz), A_ALL)
                send(slot_of(j, dx=1, fy=fy, fz=fz), A_1, to_left)
        for dx in (0, -1, 1, 2):
            send(slot_of(j, dx=dx), B_ALL, to_z)
        for dx in (0, -1, 1, 2):
            landed(slot_of(j, dx=dx, fy=True), B_ALL)
            send(slot_of(j, dx=dx, fy=True), B_ALL, to_z)

    def stage4(j):
        for fy in (False, True):
            for fz in (False, True):
                landed(slot_of(j, dx=2, fy=fy, fz=fz), A_0)
                landed(slot_of(j, dx=2, fy=fy, fz=fz), A_1)
            for dx in (0, -1, 1, 2):
                landed(slot_of(j, dx=dx, fy=fy, fz=True), B_ALL)

    v = iota((1, MAIN), 1)
    main_at = CAP * ((v >> 4) & 7) + BAND * (v >> 7) + (v & 15)
    perm_main = onehot(iota((ROWS, 1), 0) == main_at)
    u = iota((1, 128), 1)
    tail_at = CAP * ((u & 31) >> 2) + 2 * BAND + (u & 3)
    tail_match = iota((ROWS, 1), 0) == tail_at
    perm_tail = onehot(iota((ROWS, 1), 0) == tail_at)[:, 0:TAILS]

    def turn_hidden(b):
        rows = hid[ROWS * b:ROWS * b + ROWS, :]
        hmain[b] = dot(rows, perm_main, ((0,), (0,))).astype(BF16)
        spread = onehot(tail_match & ((u >> 5) == b % 4))
        part = dot(rows, spread, ((0,), (0,))).astype(BF16)
        cols = slice(128 * (b // 4), 128 * (b // 4) + 128)
        if b % 4 == 0:
            htail[:, cols] = part
        else:
            htail[:, cols] += part

    def plane_of(j, k):
        return lax.rem(2 * e + (8 - j if k == 0 else 1 + j), 8)

    t = iota((TAILS, 1), 0)
    vt = iota((1, 128), 1)
    pick_tail = [onehot(vt == 16 * (t >> 2) + 4 * q + (t & 3)) for q in range(4)]

    def unpack_tails(b):
        packed = arr[pl.ds(PLANE * b, PLANE), :, 2 * D:WIDTH].reshape(PLANE * BAND, QUARTER)
        at = pl.multiple_of(b * TAILS, TAILS)
        for q in range(4):
            utail[pl.ds(at, TAILS), q * QUARTER:(q + 1) * QUARTER] = dot(pick_tail[q], packed).astype(BF16)

    def band(b, h, c, n):
        return arr[pl.ds(PLANE * b, PLANE), :, h * D + c:h * D + c + n].reshape(PLANE * BAND, n)

    def hidden_copy(b):
        rows = pl.ds(pl.multiple_of(b * ROWS, ROWS), ROWS)
        return pltpu.make_async_remote_copy(
            src_ref=sec.at[rows], dst_ref=hout.at[rows], send_sem=hsend_sem.at[b],
            recv_sem=hrecv_sem.at[b], device_id=device(0, 0, False, -1), device_id_type=MESH)

    def section_part(b):
        at = pl.multiple_of(b * TAILS, TAILS)
        weight = w[...]
        dims = ((1,), (1,))
        low = dot(band(b, 0, 0, D), weight, dims).astype(BF16)
        high = dot(band(b, 1, 0, D), weight, dims).astype(BF16)
        tail = dot(utail[pl.ds(at, TAILS), :], weight, dims).astype(BF16)
        out = dot(perm_main[:, 0:128], low) + dot(perm_main[:, 128:256], high) + dot(perm_tail, tail)
        sec[pl.ds(pl.multiple_of(b * ROWS, ROWS), ROWS), :] = out.astype(BF16)
        hidden_copy(b).start()

    def weight_term(b, c, n):
        return (dot(hmain[b, :, 0:128], band(b, 0, c, n))
                + dot(hmain[b, :, 128:256], band(b, 1, c, n)))

    def compute(j, first, last):
        planes = [plane_of(j, k) for k in (0, 1)]
        for b in planes:
            unpack_tails(b)

        @pl.when(section > 0)
        def _():
            for b in planes:
                section_part(b)

        for c in range(0, D, 512):
            part = weight_term(planes[0], c, 512) + weight_term(planes[1], c, 512)
            if not first:
                part += acc[:, c:c + 512]
            if not last:
                acc[:, c:c + 512] = part
            else:
                part += dot(htail[...], utail[:, c:c + 512])
                wbuf[:, c:c + 512] = part.astype(BF16)
                pltpu.make_async_copy(wbuf.at[:, c:c + 512], wout.at[:, c:c + 512], out_sem.at[c // 512]).start()

    stage0(0)
    for j in (1, 2, 3):
        send_transit(j)
    hid_in.wait()
    for b in range(4):
        turn_hidden(b)
    stage1(0)
    stage0(1)
    for b in range(4, 8):
        turn_hidden(b)
    w_in.wait()
    stage2(0)
    stage1(1)
    stage0(2)
    stage2(1)
    stage3(0)
    stage1(2)
    stage0(3)
    stage2(2)
    stage3(1)
    stage1(3)
    stage2(3)
    stage4(0)
    compute(0, True, False)
    stage3(2)
    stage4(1)
    compute(1, False, False)
    stage3(3)
    stage4(2)
    compute(2, False, False)
    stage4(3)
    compute(3, False, True)

    @pl.when(section == 3)
    def _():
        hid[...] = jnp.zeros((SLOTS, UNITS), BF16)
        zero = pltpu.make_async_copy(hid, hout, loc_sem)
        zero.start()
        zero.wait()

    for c in range(0, D, 512):
        pltpu.make_async_copy(wbuf.at[:, c:c + 512], wout.at[:, c:c + 512], out_sem.at[c // 512]).wait()
    for copy in sends:
        copy.wait_send()

    @pl.when(section > 0)
    def _():
        for b in range(BLOCKS):
            hidden_copy(b).wait_send()

    @pl.when(section < 3)
    def _():
        for b in range(BLOCKS):
            hidden_copy(b).wait_recv()


def body(grad_out, expert_ids, slot_ids, gates, hidden, w_down):
    anywhere = pl.BlockSpec(memory_space=pl.ANY)
    vmem = pl.BlockSpec(memory_space=pltpu.VMEM)
    dma = pltpu.SemaphoreType.DMA
    hout, wout = pl.pallas_call(
        kernel,
        out_shape=(jax.ShapeDtypeStruct((SLOTS, UNITS), BF16), jax.ShapeDtypeStruct((UNITS, D), BF16)),
        in_specs=[vmem] * 3 + [anywhere] * 3,
        out_specs=(anywhere, anywhere),
        scratch_shapes=[
            pltpu.VMEM((BLOCKS * PLANE, BAND, WIDTH), BF16),
            pltpu.VMEM((3, BAND, WIDTH), BF16),
            pltpu.VMEM((128, D), BF16),
            pltpu.VMEM((SLOTS, UNITS), BF16),
            pltpu.VMEM((UNITS, D), BF16),
            pltpu.VMEM((BLOCKS, UNITS, MAIN), BF16),
            pltpu.VMEM((UNITS, BLOCKS * TAILS), BF16),
            pltpu.VMEM((BLOCKS * TAILS, D), BF16),
            pltpu.VMEM((UNITS, D), F32),
            pltpu.VMEM((SLOTS, UNITS), BF16),
            pltpu.VMEM((UNITS, D), BF16),
            dma((3,)), dma, dma((6,)), dma((160,)), dma((64, 4)), dma((8,)), dma((8,)),
        ],
        compiler_params=pltpu.CompilerParams(
            collective_id=0, has_side_effects=True, vmem_limit_bytes=56 * 2**20),
        cost_estimate=pl.CostEstimate(flops=15 * 10**9, bytes_accessed=12 * 10**6, transcendentals=0),
        name="dispatch_and_products",
    )(expert_ids[0].T, slot_ids[0].T, gates[0].T, grad_out[0], hidden[0], w_down[0])
    return (hout[None], wout[None])


def solution(mesh):
    in_specs = (
        P("section", ("dp", "expert"), None),
        P("section", ("dp", "expert"), None),
        P("section", ("dp", "expert"), None),
        P("section", ("dp", "expert"), None),
        P("section", None, ("dp", "expert")),
        P("section", ("dp", "expert"), None),
    )
    out_specs = (P("section", None, ("dp", "expert")), P("section", ("dp", "expert"), None))
    return jax.shard_map(body, mesh=mesh, in_specs=in_specs, out_specs=out_specs, check_vma=False)
```

time: 446 us -> 139 us (0.31)
  blocking collectives: 357 us -> 0 us
  Pallas kernels: 0 us -> 133 us
  local copies, waits for them, and re-layouts: 40.3 us -> 5.05 us
  matrix products: 25.9 us -> 0 us
  waiting for transfers between devices: 13.1 us -> 0 us
  starting transfers between devices: 6.38 us -> 0 us
    all_to_all x1 -> x0, blocking collectives: 357 us -> none  [body(): lax.all_to_all(outgoing, ('dp', 'expert'), split_axis=0, concat_axis=0, t...]
    pallas_call x0 -> x1, Pallas kernels: none -> 133 us  [body(): pl.pallas_call(kernel, out_shape=(jax.ShapeDtypeStruct((SLOTS, UNITS), BF...]
    dot_general x3 -> x0, matrix products: 25.9 us -> none  [the longest x1 13.5 us: body(): lax.dot_general(arrived, weight, (((1,), (1,)), ((), ())), preferred_elem...]
    reshape x2 -> x0, local copies, waits for them, and re-layouts: 19.3 us -> none  [the longest x1 17 us: body(): arrived = lax.all_to_all(outgoing, ('dp', 'expert'), split_axis=0, concat...]
    ppermute x1 -> x0, waiting for transfers between devices: 13.1 us -> none  [passed_along(): return lax.ppermute(block, axis, route)]
    mul x3 -> x0, local copies, waits for them, and re-layouts: 8.12 us -> none  [body(): gates[0][..., None] * grad_out[0][:, None, :].astype(jnp.float32)]
    ppermute x1 -> x0, starting transfers between devices: 6.38 us -> none  [passed_along(): return lax.ppermute(block, axis, route)]
  transfers between devices with their start and end apart: 1 -> 0, of which waited for: 1 -> 0; matrix products, arithmetic and copies ran while one was open for 3% -> 0% of each run, Pallas kernels for 0% -> 0%
where the time goes in v1:
time: 139 us
  Pallas kernels  133 us (96%)
  local copies, waits for them, and re-layouts  5.05 us (4%)
    pallas_call x1, Pallas kernels, body(): pl.pallas_call(kernel, out_shape=(jax.ShapeDtypeStruct((SLOTS, UNITS), BF...  133 us
    unnamed x4, local copies, waits for them, and re-layouts  5.05 us

profile of v1, /device:TPU:1, one launch (start us, length us, event | category | flops | bytes accessed | tf_op | source)
XLA Modules:
  0.0 138.5 jit_solution(1901325946237036045)
XLA Ops:
  0.6 132.8 %dispatch_and_products.1 = (bf16[2304,512]{1,0:T(8,128)(2,1)}, bf16[512,3072]{1,0:T(8,128)(2,1)}) custom-call(s32[2,128]{1,0:T(2,128)} %bitcast.19, s32[2,128]{1,0:T(2,128)} %bitcast.20, f32[2,128]{1,0:T(2,128)} %bitcast.21, bf16[128,3072]{1,0:T(8,128)(2,1)} %bitcast.18, bf16[2304,512]{1,0:T(8,128)(2,1)} %bitcast.17, bf16[512,3072]{1,0:T(8,128)(2,1)} %bitcast.16), custom_call_target="tpu_custom_call" | custom-call | flops 15000000512 | bytes 12000000 | tf_op jit(solution)/shard_map/dispatch_and_products/pallas_call | solution.py:352
  133.5 0.0 copy-start
  133.5 3.4 %copy.10 = bf16[1,2304,512]{2,1,0:T(8,128)(2,1)} copy(bf16[1,2304,512]{2,1,0:T(8,128)(2,1)} %bitcast.15) | data formatting | bytes 4718592
  136.9 0.0 copy-done
  136.9 1.7 %copy.11 = bf16[1,512,3072]{2,1,0:T(8,128)(2,1)} copy(bf16[1,512,3072]{2,1,0:T(8,128)(2,1)S(1)} %bitcast.14) | data formatting | bytes 6291456
Async XLA Ops:
  133.5 3.4 %copy-start = (bf16[512,3072]{1,0:T(8,128)(2,1)S(1)}, bf16[512,3072]{1,0:T(8,128)(2,1)}, u32[]{:S(2)}) copy-start(bf16[512,3072]{1,0:T(8,128)(2,1)} %get-tuple-element.5) | copy-start | bytes 9437188

commit v2 on v1

--- a/solution.py
+++ b/solution.py
@@ -24,7 +24,8 @@
 SLOTS = BLOCKS * ROWS
 MAIN = PLANE * 2 * BAND
 TAILS = PLANE * TAIL
-HALF_A = 17 * 128
+SECTION_STEP = 768
+HALF_A = 16 * 128
 HALF_B = (WIDTH - 2 * HALF_A) // 2
 A_ALL = (0, 2 * HALF_A)
 A_0 = (0, HALF_A)
@@ -32,7 +33,39 @@
 B_ALL = (2 * HALF_A, 2 * HALF_B)
 B_0 = (2 * HALF_A, HALF_B)
 B_1 = (2 * HALF_A + HALF_B, HALF_B)
-SEM_OF = {A_ALL: 0, A_0: 0, A_1: 1, B_ALL: 2, B_0: 2, B_1: 3}
+ORDER = (
+    ("A2", 0, 0), ("B3", 0, 0), ("A1", 0), ("T1",), ("T2",), ("B1R", 0), ("B1L", 0), ("A3R", 0, 0, 0),
+    ("A3L", 0, 0, 0), ("B4", 0, 0, 0), ("H", 0), ("H", 1), ("H", 2), ("H", 3), ("H", 4), ("H", 5), ("H", 6),
+    ("H", 7), ("B4", 0, 0, 1), ("B3", 0, -1), ("B3", 0, 1), ("B2R", 0), ("B2L", 0), ("A3R", 0, 1, 0),
+    ("A3L", 0, 1, 0), ("A4R", 0, 0, 0), ("A4L", 0, 0, 0), ("B4", 0, -1, 0), ("B4", 0, 1, 0), ("B3", 0, 2), ("T3",),
+    ("A2", 0, 1), ("A3R", 0, 0, 1), ("A3L", 0, 0, 1), ("A2", 1, 0), ("B1R", 1), ("B1L", 1), ("A3R", 1, 0, 0),
+    ("A3L", 1, 0, 0), ("B3", 1, 0), ("B4", 0, -1, 1), ("B4", 0, 1, 1), ("A4R", 0, 1, 0), ("A4L", 0, 1, 0),
+    ("B3", 1, -1), ("B2R", 1), ("B4", 0, 2, 0), ("B2L", 1), ("B3", 1, 1), ("A4R", 0, 0, 1), ("A4L", 0, 0, 1),
+    ("A2", 2, 0), ("A3R", 0, 1, 1), ("A3L", 0, 1, 1), ("A3R", 1, 1, 0), ("A3L", 1, 1, 0), ("C", 0, 0, 0),
+    ("B3", 1, 2), ("B4", 0, 2, 1), ("B3", 2, 0), ("C", 0, 0, 1), ("A1", 1), ("A4R", 1, 0, 0), ("A4L", 1, 0, 0),
+    ("C", 0, 0, 2), ("C", 0, 0, 3), ("B4", 1, 0, 0), ("B1R", 2), ("B1L", 2), ("A3R", 2, 0, 0), ("A3L", 2, 0, 0),
+    ("A3R", 2, 1, 0), ("A3L", 2, 1, 0), ("B4", 1, 0, 1), ("A2", 3, 0), ("B3", 3, 0), ("B4", 1, -1, 0),
+    ("B4", 1, -1, 1), ("A4R", 0, 1, 1), ("A4L", 0, 1, 1), ("A2", 1, 1), ("B3", 2, -1), ("B4", 1, 1, 0), ("B3", 2, 1),
+    ("A3R", 1, 0, 1), ("A3L", 1, 0, 1), ("A4R", 1, 1, 0), ("A4L", 1, 1, 0), ("B4", 1, 1, 1), ("B2R", 2), ("B2L", 2),
+    ("C", 0, 1, 0), ("B4", 1, 2, 0), ("A4R", 2, 0, 0), ("A4L", 2, 0, 0), ("C", 0, 1, 1), ("B4", 1, 2, 1),
+    ("C", 0, 1, 2), ("A4R", 2, 1, 0), ("A4L", 2, 1, 0), ("B4", 2, 2, 0), ("C", 0, 1, 3), ("A1", 2), ("C", 1, 0, 0),
+    ("C", 1, 0, 1), ("A3R", 1, 1, 1), ("A3L", 1, 1, 1), ("B1R", 3), ("B1L", 3), ("C", 1, 0, 2), ("C", 1, 0, 3),
+    ("A3R", 3, 0, 0), ("A3L", 3, 0, 0), ("B4", 2, 0, 0), ("B4", 2, 0, 1), ("C", 2, 0, 0), ("C", 2, 0, 1),
+    ("C", 2, 0, 2), ("C", 2, 0, 3), ("A4R", 1, 0, 1), ("A4L", 1, 0, 1), ("B4", 2, -1, 0), ("B3", 3, -1),
+    ("B3", 3, 1), ("B4", 2, -1, 1), ("A2", 2, 1), ("B4", 2, 1, 0), ("A3R", 2, 0, 1), ("A3L", 2, 0, 1),
+    ("A4R", 1, 1, 1), ("A4L", 1, 1, 1), ("B2R", 3), ("B2L", 3), ("B4", 2, 1, 1), ("A4R", 3, 0, 0), ("A4L", 3, 0, 0),
+    ("B3", 2, 2), ("A1", 3), ("A3R", 3, 1, 0), ("A3L", 3, 1, 0), ("B3", 3, 2), ("C", 1, 1, 0), ("A3R", 2, 1, 1),
+    ("A3L", 2, 1, 1), ("C", 1, 1, 1), ("C", 1, 1, 2), ("B4", 3, 0, 0), ("C", 1, 1, 3), ("A4R", 2, 0, 1),
+    ("A4L", 2, 0, 1), ("B4", 3, 0, 1), ("B4", 2, 2, 1), ("B4", 3, -1, 0), ("A4R", 3, 1, 0), ("A4L", 3, 1, 0),
+    ("A2", 3, 1), ("A3R", 3, 0, 1), ("A3L", 3, 0, 1), ("B4", 3, -1, 1), ("A4R", 2, 1, 1), ("A4L", 2, 1, 1),
+    ("B4", 3, 1, 0), ("C", 3, 0, 0), ("A3R", 3, 1, 1), ("A3L", 3, 1, 1), ("B4", 3, 1, 1), ("B4", 3, 2, 0),
+    ("C", 2, 1, 0), ("A4R", 3, 0, 1), ("A4L", 3, 0, 1), ("B4", 3, 2, 1), ("C", 2, 1, 1), ("C", 2, 1, 2),
+    ("C", 2, 1, 3), ("C", 3, 0, 1), ("C", 3, 0, 2), ("C", 3, 0, 3), ("A4R", 3, 1, 1), ("A4L", 3, 1, 1),
+    ("C", 3, 1, 0), ("C", 3, 1, 1), ("C", 3, 1, 2), ("C", 3, 1, 3),
+)
+Z_FIRST = ((2, 2),)
+WINDOW = {"xr": 3, "xl": 3, "y": 3, "zp": 3, "T": 2}
+SEM_OF = {(0, WIDTH): 0, A_ALL: 0, A_0: 0, A_1: 1, B_ALL: 2, B_0: 2, B_1: 3}
 
 
 def iota(shape, dim):
@@ -134,83 +167,91 @@
     pl.semaphore_wait(barrier, 8)
 
     sends = []
-
-    def copy_of(slot, cols, to, n):
-        piece = arr.at[slot, :, pl.ds(cols[0], cols[1])]
+    lanes = {name: [] for name in WINDOW}
+    seen = set()
+    count = iter(range(160))
+
+    def copy_of(place, cols, to, n):
+        piece = arr.at[slot_of(*place), :, pl.ds(cols[0], cols[1])]
         return pltpu.make_async_remote_copy(
             src_ref=piece, dst_ref=piece, send_sem=send_sem.at[n],
-            recv_sem=recv_sem.at[slot, SEM_OF[cols]], device_id=to, device_id_type=MESH)
-
-    def send(slot, cols, to):
-        copy = copy_of(slot, cols, to, len(sends))
+            recv_sem=recv_sem.at[slot_of(*place), SEM_OF[cols]], device_id=to, device_id_type=MESH)
+
+    def start(copy, lane):
+        queue = lanes[lane]
+        if len(queue) >= WINDOW[lane]:
+            queue.pop(0).wait_send()
         copy.start()
-        sends.append(copy)
-
-    def landed(slot, cols):
-        copy_of(slot, cols, to_z, 0).wait_recv()
+        queue.append(copy)
+
+    def send(place, cols, to, lane):
+        start(copy_of(place, cols, to, next(count)), lane)
 
     def send_transit(j):
-        copy = pltpu.make_async_remote_copy(
-            src_ref=outg.at[j - 1], dst_ref=arr.at[mine], send_sem=send_sem.at[len(sends)],
-            recv_sem=recv_sem.at[mine, 0], device_id=transit[j], device_id_type=MESH)
-        copy.start()
-        sends.append(copy)
-
-    def wait_transit(j):
-        slot = slot_of(j)
-        pltpu.make_async_remote_copy(
-            src_ref=outg.at[0], dst_ref=arr.at[slot], send_sem=send_sem.at[0],
-            recv_sem=recv_sem.at[slot, 0], device_id=to_z, device_id_type=MESH).wait_recv()
-
-    def stage0(j):
-        if j:
-            wait_transit(j)
-        send(slot_of(j), A_ALL, to_z)
-        send(slot_of(j), B_ALL, to_right)
-        send(slot_of(j), B_ALL, to_left)
-
-    def stage1(j):
-        landed(slot_of(j, fz=True), A_ALL)
-        send(slot_of(j), A_ALL, to_y)
-        send(slot_of(j, fz=True), A_ALL, to_y)
-        landed(slot_of(j, dx=-1), B_ALL)
-        send(slot_of(j, dx=-1), B_0, to_right)
-        landed(slot_of(j, dx=1), B_ALL)
-        send(slot_of(j, dx=1), B_1, to_left)
-
-    def stage2(j):
+        start(pltpu.make_async_remote_copy(
+            src_ref=outg.at[j - 1], dst_ref=arr.at[mine], send_sem=send_sem.at[next(count)],
+            recv_sem=recv_sem.at[mine, 0], device_id=transit[j], device_id_type=MESH), "T")
+
+    def need(j, dx=0, fy=False, fz=False, cols=None):
+        dx = dx % 4
+        if (dx, fy, fz) == (0, 0, 0):
+            parts = [(0, WIDTH)] if j else []
+        elif cols == A_ALL and dx == 2:
+            parts = [A_0, A_1]
+        elif cols == B_ALL and (dx, fy, fz) == (2, 0, 0):
+            parts = [B_0, B_1]
+        else:
+            parts = [cols]
+        for part in parts:
+            if (j, dx, fy, fz, part) not in seen:
+                seen.add((j, dx, fy, fz, part))
+                copy_of((j, dx, fy, fz), part, to_z, 0).wait_recv()
+
+    def issue(name, j=0, *rest):
+        if name[0] == "T":
+            send_transit(int(name[1]))
+        elif name == "A1":
+            need(j)
+            send((j,), A_ALL, to_z, "zp")
+        elif name == "A2":
+            need(j, 0, False, rest[0], A_ALL)
+            send((j, 0, False, rest[0]), A_ALL, to_y, "y")
+        elif name in ("A3R", "A3L"):
+            need(j, 0, *rest, A_ALL)
+            to, lane = (to_right, "xr") if name == "A3R" else (to_left, "xl")
+            send((j, 0, *rest), A_ALL, to, lane)
+        elif name == "A4R":
+            need(j, -1, *rest, A_ALL)
+            send((j, -1, *rest), A_0, to_right, "xr")
+        elif name == "A4L":
+            need(j, 1, *rest, A_ALL)
+            send((j, 1, *rest), A_1, to_left, "xl")
+        elif name in ("B1R", "B1L"):
+            need(j)
+            to, lane = (to_right, "xr") if name == "B1R" else (to_left, "xl")
+            send((j,), B_ALL, to, lane)
+        elif name == "B2R":
+            need(j, -1, False, False, B_ALL)
+            send((j, -1), B_0, to_right, "xr")
+        elif name == "B2L":
+            need(j, 1, False, False, B_ALL)
+            send((j, 1), B_1, to_left, "xl")
+        else:
+            dx = rest[0]
+            z_first = (j, dx % 4) in Z_FIRST
+            other = len(rest) > 1 and rest[1]
+            place = (j, dx, False, other) if z_first else (j, dx, other, False)
+            need(*place, B_ALL)
+            if (name == "B3") == z_first:
+                send(place, B_ALL, to_z, "zp")
+            else:
+                send(place, B_ALL, to_y, "y")
+
+    def need_plane(j, fz):
         for fy in (False, True):
-            for fz in (False, True):
-                if fy:
-                    landed(slot_of(j, fy=True, fz=fz), A_ALL)
-                send(slot_of(j, fy=fy, fz=fz), A_ALL, to_right)
-                send(slot_of(j, fy=fy, fz=fz), A_ALL, to_left)
-        for dx in (0, -1, 1):
-            send(slot_of(j, dx=dx), B_ALL, to_y)
-        landed(slot_of(j, dx=2), B_0)
-        landed(slot_of(j, dx=2), B_1)
-        send(slot_of(j, dx=2), B_ALL, to_y)
-
-    def stage3(j):
-        for fy in (False, True):
-            for fz in (False, True):
-                landed(slot_of(j, dx=-1, fy=fy, fz=fz), A_ALL)
-                send(slot_of(j, dx=-1, fy=fy, fz=fz), A_0, to_right)
-                landed(slot_of(j, dx=1, fy=fy, fz=fz), A_ALL)
-                send(slot_of(j, dx=1, fy=fy, fz=fz), A_1, to_left)
-        for dx in (0, -1, 1, 2):
-            send(slot_of(j, dx=dx), B_ALL, to_z)
-        for dx in (0, -1, 1, 2):
-            landed(slot_of(j, dx=dx, fy=True), B_ALL)
-            send(slot_of(j, dx=dx, fy=True), B_ALL, to_z)
-
-    def stage4(j):
-        for fy in (False, True):
-            for fz in (False, True):
-                landed(slot_of(j, dx=2, fy=fy, fz=fz), A_0)
-                landed(slot_of(j, dx=2, fy=fy, fz=fz), A_1)
-            for dx in (0, -1, 1, 2):
-                landed(slot_of(j, dx=dx, fy=fy, fz=True), B_ALL)
+            for dx in range(4):
+                need(j, dx, fy, fz, A_ALL)
+                need(j, dx, fy, fz, B_ALL)
 
     v = iota((1, MAIN), 1)
     main_at = CAP * ((v >> 4) & 7) + BAND * (v >> 7) + (v & 15)
@@ -231,9 +272,6 @@
         else:
             htail[:, cols] += part
 
-    def plane_of(j, k):
-        return lax.rem(2 * e + (8 - j if k == 0 else 1 + j), 8)
-
     t = iota((TAILS, 1), 0)
     vt = iota((1, 128), 1)
     pick_tail = [onehot(vt == 16 * (t >> 2) + 4 * q + (t & 3)) for q in range(4)]
@@ -255,72 +293,58 @@
 
     def section_part(b):
         at = pl.multiple_of(b * TAILS, TAILS)
-        weight = w[...]
-        dims = ((1,), (1,))
-        low = dot(band(b, 0, 0, D), weight, dims).astype(BF16)
-        high = dot(band(b, 1, 0, D), weight, dims).astype(BF16)
-        tail = dot(utail[pl.ds(at, TAILS), :], weight, dims).astype(BF16)
-        out = dot(perm_main[:, 0:128], low) + dot(perm_main[:, 128:256], high) + dot(perm_tail, tail)
+        out = jnp.zeros((MAIN + TAILS, UNITS), F32)
+        for c in range(0, D, SECTION_STEP):
+            rows = jnp.concatenate(
+                [band(b, 0, c, SECTION_STEP), band(b, 1, c, SECTION_STEP),
+                 utail[pl.ds(at, TAILS), c:c + SECTION_STEP]], axis=0)
+            out += dot(rows, w[:, c:c + SECTION_STEP], ((1,), (1,)))
+        out = out.astype(BF16)
+        out = dot(perm_main, out[0:MAIN]) + dot(perm_tail, out[MAIN:])
         sec[pl.ds(pl.multiple_of(b * ROWS, ROWS), ROWS), :] = out.astype(BF16)
         hidden_copy(b).start()
 
-    def weight_term(b, c, n):
-        return (dot(hmain[b, :, 0:128], band(b, 0, c, n))
-                + dot(hmain[b, :, 128:256], band(b, 1, c, n)))
-
-    def compute(j, first, last):
-        planes = [plane_of(j, k) for k in (0, 1)]
-        for b in planes:
+    def weight_part(b, c, n, first, last):
+        rows = jnp.concatenate([band(b, 0, c, n), band(b, 1, c, n)], axis=0)
+        part = dot(hmain[b], rows)
+        if not first:
+            part += acc[:, c:c + n]
+        if not last:
+            acc[:, c:c + n] = part
+        else:
+            part += dot(htail[...], utail[:, c:c + n])
+            wbuf[:, c:c + n] = part.astype(BF16)
+            pltpu.make_async_copy(wbuf.at[:, c:c + n], wout.at[:, c:c + n], out_sem.at[c // n]).start()
+
+    def compute(j, fz, piece):
+        fz = bool(fz)
+        b = lax.div(slot_of(j, 0, False, fz), PLANE)
+        if piece == 0:
+            need_plane(j, fz)
             unpack_tails(b)
 
-        @pl.when(section > 0)
-        def _():
-            for b in planes:
+            @pl.when(section > 0)
+            def _():
                 section_part(b)
-
-        for c in range(0, D, 512):
-            part = weight_term(planes[0], c, 512) + weight_term(planes[1], c, 512)
-            if not first:
-                part += acc[:, c:c + 512]
-            if not last:
-                acc[:, c:c + 512] = part
-            else:
-                part += dot(htail[...], utail[:, c:c + 512])
-                wbuf[:, c:c + 512] = part.astype(BF16)
-                pltpu.make_async_copy(wbuf.at[:, c:c + 512], wout.at[:, c:c + 512], out_sem.at[c // 512]).start()
-
-    stage0(0)
-    for j in (1, 2, 3):
-        send_transit(j)
-    hid_in.wait()
-    for b in range(4):
-        turn_hidden(b)
-    stage1(0)
-    stage0(1)
-    for b in range(4, 8):
-        turn_hidden(b)
-    w_in.wait()
-    stage2(0)
-    stage1(1)
-    stage0(2)
-    stage2(1)
-    stage3(0)
-    stage1(2)
-    stage0(3)
-    stage2(2)
-    stage3(1)
-    stage1(3)
-    stage2(3)
-    stage4(0)
-    compute(0, True, False)
-    stage3(2)
-    stage4(1)
-    compute(1, False, False)
-    stage3(3)
-    stage4(2)
-    compute(2, False, False)
-    stage4(3)
-    compute(3, False, True)
+        else:
+            for c in (0, 512):
+                at = (piece - 1) * 1024 + c
+                weight_part(b, at, 512, (j, fz) == planes[0], (j, fz) == planes[-1])
+
+    planes = [(step[1], bool(step[2])) for step in ORDER if step[0] == "C" and step[3] == 0]
+    for step in ORDER:
+        if step[0] == "H":
+            if step[1] == 0:
+                hid_in.wait()
+            turn_hidden(step[1])
+        elif step[0] == "C":
+            if step[1:3] == planes[0] and step[3] == 0:
+                w_in.wait()
+            compute(*step[1:])
+        else:
+            issue(*step)
+    for queue in lanes.values():
+        sends.extend(queue)
 
     @pl.when(section == 3)
     def _():

time: 139 us -> 115 us (0.83)
  Pallas kernels: 133 us -> 110 us
    pallas_call x1, Pallas kernels: 133 us -> 110 us  [body(): pl.pallas_call(kernel, out_shape=(jax.ShapeDtypeStruct((SLOTS, UNITS), BF...]
where the time goes in v2:
time: 115 us
  Pallas kernels  110 us (96%)
  local copies, waits for them, and re-layouts  5.05 us (4%)
    pallas_call x1, Pallas kernels, body(): pl.pallas_call(kernel, out_shape=(jax.ShapeDtypeStruct((SLOTS, UNITS), BF...  110 us
    unnamed x4, local copies, waits for them, and re-layouts  5.05 us

profile of v2, /device:TPU:1, one launch (start us, length us, event | category | flops | bytes accessed | tf_op | source)
XLA Modules:
  0.0 115.2 jit_solution(7938581914537240370)
XLA Ops:
  0.6 109.5 %dispatch_and_products.1 = (bf16[2304,512]{1,0:T(8,128)(2,1)}, bf16[512,3072]{1,0:T(8,128)(2,1)}) custom-call(s32[2,128]{1,0:T(2,128)} %bitcast.19, s32[2,128]{1,0:T(2,128)} %bitcast.20, f32[2,128]{1,0:T(2,128)} %bitcast.21, bf16[128,3072]{1,0:T(8,128)(2,1)} %bitcast.18, bf16[2304,512]{1,0:T(8,128)(2,1)} %bitcast.17, bf16[512,3072]{1,0:T(8,128)(2,1)} %bitcast.16), custom_call_target="tpu_custom_call" | custom-call | flops 15000000512 | bytes 12000000 | tf_op jit(solution)/shard_map/dispatch_and_products/pallas_call | solution.py:376
  110.2 0.0 copy-start
  110.2 3.4 %copy.10 = bf16[1,2304,512]{2,1,0:T(8,128)(2,1)} copy(bf16[1,2304,512]{2,1,0:T(8,128)(2,1)} %bitcast.15) | data formatting | bytes 4718592
  113.6 0.0 copy-done
  113.6 1.7 %copy.11 = bf16[1,512,3072]{2,1,0:T(8,128)(2,1)} copy(bf16[1,512,3072]{2,1,0:T(8,128)(2,1)S(1)} %bitcast.14) | data formatting | bytes 6291456
Async XLA Ops:
  110.2 3.4 %copy-start = (bf16[512,3072]{1,0:T(8,128)(2,1)S(1)}, bf16[512,3072]{1,0:T(8,128)(2,1)}, u32[]{:S(2)}) copy-start(bf16[512,3072]{1,0:T(8,128)(2,1)} %get-tuple-element.5) | copy-start | bytes 9437188

commit v3 on v2

v3 whole, which is shorter than its diff:
```python
import functools

import jax
import jax.numpy as jnp
from jax import lax
from jax.experimental import pallas as pl
from jax.experimental.pallas import tpu as pltpu
from jax.sharding import PartitionSpec as P

MESH = pl.DeviceIdType.MESH
FLIGHT = 4
BF16, F32, I32 = jnp.bfloat16, jnp.float32, jnp.int32

D = 3072
CAP = 36
BAND = 16
TAIL = CAP - 2 * BAND
QUARTER = D // 4
WIDTH = 2 * D + QUARTER
UNITS = 512
BLOCKS = 8
PLANE = 8
ROWS = PLANE * CAP
SLOTS = BLOCKS * ROWS
MAIN = PLANE * 2 * BAND
TAILS = PLANE * TAIL
SECTION_STEP = 768
HALF_A = 16 * 128
HALF_B = (WIDTH - 2 * HALF_A) // 2
A_ALL = (0, 2 * HALF_A)
A_0 = (0, HALF_A)
A_1 = (HALF_A, HALF_A)
B_ALL = (2 * HALF_A, 2 * HALF_B)
B_0 = (2 * HALF_A, HALF_B)
B_1 = (2 * HALF_A + HALF_B, HALF_B)
ORDER = (
    ("A2", 0, 0), ("A1", 0), ("B1R", 0), ("B1L", 0), ("B3", 0, 0), ("A3R", 0, 0, 0), ("A3L", 0, 0, 0),
    ("B4", 0, 0, 0), ("H", 0), ("T1",), ("H", 1), ("H", 2), ("H", 3), ("H", 4), ("H", 5), ("H", 6), ("H", 7),
    ("B3", 0, -1), ("B3", 0, 1), ("B2R", 0), ("B2L", 0), ("B4", 0, -1, 0), ("B4", 0, 0, 1), ("A3R", 0, 1, 0),
    ("A2", 0, 1), ("T2",), ("A3L", 0, 0, 1), ("A3R", 0, 0, 1), ("A3L", 0, 1, 0), ("B3", 0, 2), ("A2", 1, 0),
    ("A1", 1), ("B4", 0, 1, 0), ("B1R", 1), ("B1L", 1), ("A4R", 0, 0, 0), ("A4L", 0, 0, 0), ("B3", 1, 0),
    ("A4R", 0, 0, 1), ("A4L", 0, 0, 1), ("A4R", 0, 1, 0), ("A4L", 0, 1, 0), ("B3", 1, -1), ("B4", 0, -1, 1),
    ("B2R", 1), ("B2L", 1), ("A3R", 0, 1, 1), ("A3L", 0, 1, 1), ("B3", 1, 1), ("B4", 0, 1, 1), ("A3R", 1, 0, 0),
    ("A3L", 1, 0, 0), ("C", 0, 0, 0), ("T3",), ("A2", 1, 1), ("C", 0, 0, 1), ("B3", 1, 2), ("C", 0, 0, 2), ("A1", 2),
    ("C", 0, 0, 3), ("A2", 2, 0), ("B1R", 2), ("B1L", 2), ("B4", 0, 2, 0), ("A4R", 0, 1, 1), ("A4L", 0, 1, 1),
    ("A3R", 1, 0, 1), ("B3", 2, 0), ("A3L", 1, 0, 1), ("A3R", 1, 1, 0), ("A3L", 1, 1, 0), ("B3", 2, -1),
    ("B4", 0, 2, 1), ("B4", 1, 0, 0), ("A2", 2, 1), ("B2R", 2), ("B2L", 2), ("A3R", 1, 1, 1), ("B3", 2, 1),
    ("A3L", 1, 1, 1), ("A4R", 1, 0, 0), ("A4L", 1, 0, 0), ("B4", 1, 0, 1), ("B4", 1, -1, 0), ("B3", 2, 2),
    ("C", 0, 1, 0), ("B1R", 3), ("B1L", 3), ("C", 0, 1, 1), ("A4R", 1, 0, 1), ("A4L", 1, 0, 1), ("A2", 3, 0),
    ("C", 0, 1, 2), ("A1", 3), ("C", 0, 1, 3), ("B3", 3, 0), ("B4", 1, -1, 1), ("A4R", 1, 1, 0), ("A4L", 1, 1, 0),
    ("A4R", 1, 1, 1), ("A4L", 1, 1, 1), ("B3", 3, -1), ("B4", 1, 1, 0), ("B2R", 3), ("B2L", 3), ("A3R", 2, 0, 0),
    ("B4", 1, 1, 1), ("A3L", 2, 0, 0), ("B3", 3, 1), ("C", 1, 0, 0), ("A3R", 2, 0, 1), ("A2", 3, 1),
    ("A3L", 2, 0, 1), ("C", 1, 0, 1), ("B4", 1, 2, 0), ("C", 1, 0, 2), ("C", 1, 0, 3), ("B4", 1, 2, 1), ("B3", 3, 2),
    ("A3R", 2, 1, 0), ("A3L", 2, 1, 0), ("B4", 2, 0, 0), ("B4", 2, 0, 1), ("A3R", 2, 1, 1), ("A3L", 2, 1, 1),
    ("C", 1, 1, 0), ("A4R", 2, 0, 0), ("A4L", 2, 0, 0), ("B4", 2, -1, 0), ("C", 1, 1, 1), ("C", 1, 1, 2),
    ("C", 1, 1, 3), ("B4", 2, -1, 1), ("A4R", 2, 0, 1), ("A4L", 2, 0, 1), ("A4R", 2, 1, 0), ("A4L", 2, 1, 0),
    ("B4", 2, 1, 0), ("B4", 2, 1, 1), ("A4R", 2, 1, 1), ("A4L", 2, 1, 1), ("A3R", 3, 0, 0), ("A3L", 3, 0, 0),
    ("C", 2, 0, 0), ("B4", 2, 2, 0), ("B4", 2, 2, 1), ("A3R", 3, 0, 1), ("A3L", 3, 0, 1), ("C", 2, 0, 1),
    ("C", 2, 0, 2), ("C", 2, 0, 3), ("A3R", 3, 1, 0), ("A3L", 3, 1, 0), ("B4", 3, 0, 0), ("B4", 3, 0, 1),
    ("C", 2, 1, 0), ("A3R", 3, 1, 1), ("A3L", 3, 1, 1), ("C", 2, 1, 1), ("C", 2, 1, 2), ("A4R", 3, 0, 0),
    ("A4L", 3, 0, 0), ("B4", 3, -1, 0), ("B4", 3, -1, 1), ("C", 2, 1, 3), ("C", 3, 0, 0), ("A4R", 3, 0, 1),
    ("A4L", 3, 0, 1), ("B4", 3, 1, 0), ("B4", 3, 1, 1), ("A4R", 3, 1, 0), ("A4L", 3, 1, 0), ("A4R", 3, 1, 1),
    ("A4L", 3, 1, 1), ("B4", 3, 2, 0), ("B4", 3, 2, 1), ("C", 3, 0, 1), ("C", 3, 0, 2), ("C", 3, 0, 3),
    ("C", 3, 0, 4), ("C", 3, 1, 0), ("C", 3, 1, 1), ("C", 3, 1, 2), ("C", 3, 1, 3), ("C", 3, 1, 4),
)
SPLIT = ((3, False), (3, True))
Y_FIRST = ()
Z_FIRST = ()
WINDOW = {"xr": 8, "xl": 8, "y": 8, "zp": 8, "T": 8}
SEM_OF = {(0, WIDTH): 0, A_ALL: 0, A_0: 0, A_1: 1, B_ALL: 2, B_0: 2, B_1: 3}


def iota(shape, dim):
    return lax.broadcasted_iota(I32, shape, dim)


def onehot(cond):
    return cond.astype(F32).astype(BF16)


def dot(a, b, dims=((1,), (0,))):
    return lax.dot_general(a, b, (dims, ((), ())), preferred_element_type=F32)


def kernel(ids_ref, slots_ref, gates_ref, grad_hbm, hid_hbm, w_hbm, hout, wout,
           arr, outg, grad, hid, w, hmain, htail, utail, acc, sec,
           in_sem, send_sem, recv_sem, hsend_sem, hrecv_sem):
    section = lax.axis_index("section")
    z = lax.axis_index("dp")
    xy = lax.axis_index("expert")
    x, yh = lax.div(xy, 2), lax.rem(xy, 2)
    zb = lax.rem(z, 2)
    e = lax.div(z, 2)
    sg = 2 * zb - 1

    grad_in = pltpu.make_async_copy(grad_hbm, grad, in_sem.at[0])
    grad_in.start()
    hid_in = pltpu.make_async_copy(hid_hbm, hid, in_sem.at[1])
    hid_in.start()
    w_in = pltpu.make_async_copy(w_hbm, w, in_sem.at[2])
    w_in.start()

    def device(dz, dx, flip, ds=0):
        to_y = 1 - yh if flip else yh
        return (section + ds, lax.rem(z + dz + 8, 8), lax.rem(x + dx + 4, 4) * 2 + to_y)

    zflip = 1 - 2 * zb
    to_z = device(zflip, 0, False)
    to_y = device(0, 0, True)
    to_right = device(0, 1, False)
    to_left = device(0, -1, False)
    transit = {1: device(sg, 0, False), 2: device(-2 * sg, 0, False), 3: device(3 * sg, 0, False)}
    transit_from = {1: transit[1], 2: device(2 * sg, 0, False), 3: transit[3]}

    barrier = pltpu.get_barrier_semaphore()
    after = (lax.rem(section + 1, 4), z, xy)
    for other in (to_z, to_y, to_right, to_left, transit_from[1], transit_from[2], transit_from[3], after):
        pl.semaphore_signal(barrier, inc=1, device_id=other, device_id_type=MESH)

    def chunk_expert(j):
        return lax.rem(e + {0: 0, 1: sg, 2: -sg, 3: 2}[j] + 4, 4)

    experts = [chunk_expert(j) for j in range(4)]

    def expert_rows(j):
        base = jnp.full(j.shape, experts[3] * CAP, I32)
        for k in (2, 1, 0):
            base = jnp.where(j == k, experts[k] * CAP, base)
        return base

    def slot_of(j, dx=0, fy=False, fz=False):
        tz = z + zflip if fz else z
        tsg = -sg if fz else sg
        ty = 1 - yh if fy else yh
        return lax.rem(tz + tsg * j + 8, 8) * PLANE + lax.rem(x + dx + 4, 4) * 2 + ty

    place = ids_ref[...] * CAP + slots_ref[...]
    place0, place1 = place[0:1, :], place[1:2, :]
    gate0, gate1 = gates_ref[0:1, :], gates_ref[1:2, :]
    mine = slot_of(0)

    def match(want):
        hit0, hit1 = place0 == want, place1 == want
        gate = jnp.sum(jnp.where(hit0, gate0, 0.0) + jnp.where(hit1, gate1, 0.0), axis=1, keepdims=True)
        return hit0 | hit1, gate

    def pack(rounds):
        n = len(rounds)
        targets = [arr.at[mine] if j == 0 else outg.at[j - 1] for j in rounds]
        m = iota((BAND * n, 1), 0)
        base = expert_rows((m >> 4) + rounds[0])
        for h in range(2):
            hit, gate = match(base + BAND * h + (m & 15))
            pick = onehot(hit)
            for c in range(0, D, 512):
                part = (dot(pick, grad[:, c:c + 512]) * gate).astype(BF16)
                for k in range(n):
                    targets[k][:, h * D + c:h * D + c + 512] = part[BAND * k:BAND * (k + 1)]
        hit, gate = match(base + 2 * BAND + (m & 3))
        part = jnp.zeros((BAND * n, QUARTER), F32)
        for q in range(4):
            part += dot(onehot(hit & (((m >> 2) & 3) == q)), grad[:, q * QUARTER:(q + 1) * QUARTER])
        part = (part * gate).astype(BF16)
        for k in range(n):
            targets[k][:, 2 * D:WIDTH] = part[BAND * k:BAND * (k + 1)]

    grad_in.wait()
    pack((0,))
    pl.semaphore_wait(barrier, 8)

    sends = []
    lanes = {name: [] for name in WINDOW}
    seen = set()
    count = iter(range(160))

    def copy_of(place, cols, to, n):
        piece = arr.at[slot_of(*place), :, pl.ds(cols[0], cols[1])]
        return pltpu.make_async_remote_copy(
            src_ref=piece, dst_ref=piece, send_sem=send_sem.at[n],
            recv_sem=recv_sem.at[slot_of(*place), SEM_OF[cols]], device_id=to, device_id_type=MESH)

    def start(copy, lane):
        queue = lanes[lane]
        if len(queue) >= WINDOW[lane]:
            queue.pop(0).wait_send()
        copy.start()
        queue.append(copy)

    def send(place, cols, to, lane):
        start(copy_of(place, cols, to, next(count)), lane)

    def send_transit(j):
        start(pltpu.make_async_remote_copy(
            src_ref=outg.at[j - 1], dst_ref=arr.at[mine], send_sem=send_sem.at[next(count)],
            recv_sem=recv_sem.at[mine, 0], device_id=transit[j], device_id_type=MESH), "T")

    def need(j, dx=0, fy=False, fz=False, cols=None):
        dx = dx % 4
        if (dx, fy, fz) == (0, 0, 0):
            parts = [(0, WIDTH)] if j else []
        elif cols == A_ALL and dx == 2:
            parts = [A_0, A_1]
        elif cols == B_ALL and (dx, fy, fz) == (2, 0, 0):
            parts = [B_0, B_1]
        else:
            parts = [cols]
        for part in parts:
            if (j, dx, fy, fz, part) not in seen:
                seen.add((j, dx, fy, fz, part))
                copy_of((j, dx, fy, fz), part, to_z, 0).wait_recv()

    def issue(name, j=0, *rest):
        if name[0] == "T":
            send_transit(int(name[1]))
        elif name == "A1":
            need(j)
            if j in Y_FIRST:
                send((j,), A_ALL, to_y, "y")
            else:
                send((j,), A_ALL, to_z, "zp")
        elif name == "A2" and j in Y_FIRST:
            need(j, 0, rest[0], False, A_ALL)
            send((j, 0, rest[0], False), A_ALL, to_z, "zp")
        elif name == "A2":
            need(j, 0, False, rest[0], A_ALL)
            send((j, 0, False, rest[0]), A_ALL, to_y, "y")
        elif name in ("A3R", "A3L"):
            need(j, 0, *rest, A_ALL)
            to, lane = (to_right, "xr") if name == "A3R" else (to_left, "xl")
            send((j, 0, *rest), A_ALL, to, lane)
        elif name == "A4R":
            need(j, -1, *rest, A_ALL)
            send((j, -1, *rest), A_0, to_right, "xr")
        elif name == "A4L":
            need(j, 1, *rest, A_ALL)
            send((j, 1, *rest), A_1, to_left, "xl")
        elif name in ("B1R", "B1L"):
            need(j)
            to, lane = (to_right, "xr") if name == "B1R" else (to_left, "xl")
            send((j,), B_ALL, to, lane)
        elif name == "B2R":
            need(j, -1, False, False, B_ALL)
            send((j, -1), B_0, to_right, "xr")
        elif name == "B2L":
            need(j, 1, False, False, B_ALL)
            send((j, 1), B_1, to_left, "xl")
        else:
            dx = rest[0]
            z_first = (j, dx % 4) in Z_FIRST
            other = len(rest) > 1 and rest[1]
            place = (j, dx, False, other) if z_first else (j, dx, other, False)
            need(*place, B_ALL)
            if (name == "B3") == z_first:
                send(place, B_ALL, to_z, "zp")
            else:
                send(place, B_ALL, to_y, "y")

    def need_plane(j, fz, far):
        for fy in (False, True):
            for dx in (0, 1, 3, 2) if far else (0, 1, 3):
                need(j, dx, fy, fz, A_ALL)
                need(j, dx, fy, fz, B_ALL)

    v = iota((1, MAIN), 1)
    main_at = CAP * ((v >> 4) & 7) + BAND * (v >> 7) + (v & 15)
    perm_main = onehot(iota((ROWS, 1), 0) == main_at)
    u = iota((1, 128), 1)
    tail_at = CAP * ((u & 31) >> 2) + 2 * BAND + (u & 3)
    tail_match = iota((ROWS, 1), 0) == tail_at
    perm_tail = onehot(iota((ROWS, 1), 0) == tail_at)[:, 0:TAILS]

    def turn_hidden(b):
        rows = hid[ROWS * b:ROWS * b + ROWS, :]
        hmain[b] = dot(rows, perm_main, ((0,), (0,))).astype(BF16)
        spread = onehot(tail_match & ((u >> 5) == b % 4))
        part = dot(rows, spread, ((0,), (0,))).astype(BF16)
        cols = slice(128 * (b // 4), 128 * (b // 4) + 128)
        if b % 4 == 0:
            htail[:, cols] = part
        else:
            htail[:, cols] += part

    def perms(sources):
        at = iota((sources * CAP, 1), 0)
        p = iota((1, sources * 2 * BAND), 1)
        main = onehot(at == CAP * ((p >> 4) & (sources - 1)) + BAND * (p >> (4 + sources.bit_length() - 1)) + (p & 15))
        q = iota((1, 128), 1)
        tail = onehot(at == CAP * (q >> 2) + 2 * BAND + (q & 3))[:, 0:sources * TAIL]
        return main, tail

    perms_whole, perms_half = perms(PLANE), perms(PLANE // 2)

    def unpack_tails(start, sources):
        packed = arr[pl.ds(start, sources), :, 2 * D:WIDTH].reshape(sources * BAND, QUARTER)
        t = iota((sources * TAIL, 1), 0)
        v = iota((1, sources * BAND), 1)
        rows = pl.ds(pl.multiple_of(start * TAIL, BAND), sources * TAIL)
        for q in range(4):
            pick = onehot(v == BAND * (t >> 2) + 4 * q + (t & 3))
            utail[rows, q * QUARTER:(q + 1) * QUARTER] = dot(pick, packed).astype(BF16)

    def band(b, h, c, n):
        return arr[pl.ds(PLANE * b, PLANE), :, h * D + c:h * D + c + n].reshape(PLANE * BAND, n)

    def hidden_copy(b, side, at, rows):
        piece = pl.ds(pl.multiple_of(at, BAND), rows)
        return pltpu.make_async_remote_copy(
            src_ref=sec.at[piece], dst_ref=hout.at[piece], send_sem=hsend_sem.at[b, side],
            recv_sem=hrecv_sem.at[b, side], device_id=device(0, 0, False, -1), device_id_type=MESH)

    def pair_of(side):
        near = lax.div(x, 2)
        return 1 - near if side else near

    def plane_at(plane):
        return lax.div(slot_of(plane[0], 0, False, plane[1]), PLANE)

    def hidden_copies(plane, sides=(0, 1)):
        b = plane_at(plane)
        if plane in SPLIT:
            return [hidden_copy(b, side, b * ROWS + pair_of(side) * (ROWS // 2), ROWS // 2) for side in sides]
        return [hidden_copy(b, 0, b * ROWS, ROWS)]

    def section_part(b, start, sources, perms):
        mains, tails = sources * 2 * BAND, sources * TAIL
        rows = jnp.concatenate(
            [arr[pl.ds(start, sources), :, 0:D].reshape(mains // 2, D),
             arr[pl.ds(start, sources), :, D:2 * D].reshape(mains // 2, D),
             utail[pl.ds(pl.multiple_of(start * TAIL, BAND), tails), :]], axis=0)
        out = dot(rows, w[...], ((1,), (1,))).astype(BF16)
        out = dot(perms[0], out[0:mains]) + dot(perms[1], out[mains:])
        sec[pl.ds(pl.multiple_of(start * CAP, BAND), sources * CAP), :] = out.astype(BF16)

    def weight_part(b, c, n, first, last):
        rows = jnp.concatenate([band(b, 0, c, n), band(b, 1, c, n)], axis=0)
        part = dot(hmain[b], rows)
        if not first:
            part += acc[:, c:c + n]
        if not last:
            acc[:, c:c + n] = part
        else:
            part += dot(htail[...], utail[:, c:c + n])
            wout[:, c:c + n] = part.astype(BF16)

    def compute(j, fz, piece):
        plane = (j, bool(fz))
        b = plane_at(plane)
        sections = 2 if plane in SPLIT else 1
        if piece < sections:
            need_plane(*plane, far=piece == sections - 1)
            start = b * PLANE
            if sections == 2:
                start = start + pair_of(piece) * (PLANE // 2)
            unpack_tails(start, PLANE // sections)

            @pl.when(section > 0)
            def _():
                section_part(b, start, PLANE // sections, perms_half if sections == 2 else perms_whole)
                hidden_copies(plane, (piece,))[0].start()
        else:
            for c in (0, 512):
                at = (piece - sections) * 1024 + c
                weight_part(b, at, 512, plane == planes[0], plane == planes[-1])

    planes = [(step[1], bool(step[2])) for step in ORDER if step[0] == "C" and step[3] == 0]
    for step in ORDER:
        if step[0] == "H":
            if step[1] == 0:
                hid_in.wait()
            turn_hidden(step[1])
        elif step[0] == "C":
            if step[1:3] == planes[0] and step[3] == 0:
                w_in.wait()
            compute(*step[1:])
        else:
            if step == ("T1",):
                pack((1, 2, 3))
            issue(*step)
    for queue in lanes.values():
        sends.extend(queue)

    @pl.when(section == 3)
    def _():
        hout[...] = jnp.zeros((SLOTS, UNITS), BF16)

    for copy in sends:
        copy.wait_send()

    @pl.when(section > 0)
    def _():
        for plane in planes:
            for copy in hidden_copies(plane):
                copy.wait_send()

    @pl.when(section < 3)
    def _():
        for plane in planes:
            for copy in hidden_copies(plane):
                copy.wait_recv()


def body(grad_out, expert_ids, slot_ids, gates, hidden, w_down):
    anywhere = pl.BlockSpec(memory_space=pl.ANY)
    vmem = pl.BlockSpec(memory_space=pltpu.VMEM)
    dma = pltpu.SemaphoreType.DMA
    hout, wout = pl.pallas_call(
        kernel,
        out_shape=(pltpu.VMEM((SLOTS, UNITS), BF16), pltpu.VMEM((UNITS, D), BF16)),
        in_specs=[vmem] * 3 + [anywhere] * 3,
        out_specs=(vmem, vmem),
        scratch_shapes=[
            pltpu.VMEM((BLOCKS * PLANE, BAND, WIDTH), BF16),
            pltpu.VMEM((3, BAND, WIDTH), BF16),
            pltpu.VMEM((128, D), BF16),
            pltpu.VMEM((SLOTS, UNITS), BF16),
            pltpu.VMEM((UNITS, D), BF16),
            pltpu.VMEM((BLOCKS, UNITS, MAIN), BF16),
            pltpu.VMEM((UNITS, BLOCKS * TAILS), BF16),
            pltpu.VMEM((BLOCKS * TAILS, D), BF16),
            pltpu.VMEM((UNITS, D), F32),
            pltpu.VMEM((SLOTS, UNITS), BF16),
            dma((3,)), dma((160,)), dma((64, 4)), dma((8, 2)), dma((8, 2)),
        ],
        compiler_params=pltpu.CompilerParams(
            collective_id=0, has_side_effects=True, vmem_limit_bytes=54 * 2**20),
        cost_estimate=pl.CostEstimate(flops=15 * 10**9, bytes_accessed=12 * 10**6, transcendentals=0),
        name="dispatch_and_products",
    )(expert_ids[0].T, slot_ids[0].T, gates[0].T, grad_out[0], hidden[0], w_down[0])
    return (hout[None], wout[None])


def solution(mesh):
    in_specs = (
        P("section", ("dp", "expert"), None),
        P("section", ("dp", "expert"), None),
        P("section", ("dp", "expert"), None),
        P("section", ("dp", "expert"), None),
        P("section", None, ("dp", "expert")),
        P("section", ("dp", "expert"), None),
    )
    out_specs = (P("section", None, ("dp", "expert")), P("section", ("dp", "expert"), None))
    return jax.shard_map(body, mesh=mesh, in_specs=in_specs, out_specs=out_specs, check_vma=False)
```

time: 115 us -> 111 us (0.965)
  Pallas kernels: 110 us -> 107 us
  local copies, waits for them, and re-layouts: 5.05 us -> 3.07 us
    pallas_call x1, Pallas kernels: 110 us -> 107 us  [body(): pl.pallas_call(kernel, out_shape=(pltpu.VMEM((SLOTS, UNITS), BF16), pltpu...]
    unnamed x4 -> x2, local copies, waits for them, and re-layouts: 5.05 us -> 3.07 us
where the time goes in v3:
time: 111 us
  Pallas kernels  107 us (96%)
  local copies, waits for them, and re-layouts  3.07 us (3%)
    pallas_call x1, Pallas kernels, body(): pl.pallas_call(kernel, out_shape=(pltpu.VMEM((SLOTS, UNITS), BF16), pltpu...  107 us
    unnamed x2, local copies, waits for them, and re-layouts  3.07 us

profile of v3, /device:TPU:1, one launch (start us, length us, event | category | flops | bytes accessed | tf_op | source)
XLA Modules:
  0.0 111.1 jit_solution(5141428472268640044)
XLA Ops:
  0.6 107.4 %dispatch_and_products.1 = (bf16[2304,512]{1,0:T(8,128)(2,1)S(1)}, bf16[512,3072]{1,0:T(8,128)(2,1)S(1)}) custom-call(s32[2,128]{1,0:T(2,128)} %bitcast.19, s32[2,128]{1,0:T(2,128)} %bitcast.20, f32[2,128]{1,0:T(2,128)} %bitcast.21, bf16[128,3072]{1,0:T(8,128)(2,1)} %bitcast.18, bf16[2304,512]{1,0:T(8,128)(2,1)} %bitcast.17, bf16[512,3072]{1,0:T(8,128)(2,1)} %bitcast.16), custom_call_target="tpu_custom_call" | custom-call | flops 15000000512 | bytes 12000000 | tf_op jit(solution)/shard_map/dispatch_and_products/pallas_call | solution.py:406
  108.0 1.4 %copy.10 = bf16[1,2304,512]{2,1,0:T(8,128)(2,1)} copy(bf16[1,2304,512]{2,1,0:T(8,128)(2,1)S(1)} %bitcast.15) | data formatting | bytes 4718592
  109.4 1.7 %copy.11 = bf16[1,512,3072]{2,1,0:T(8,128)(2,1)} copy(bf16[1,512,3072]{2,1,0:T(8,128)(2,1)S(1)} %bitcast.14) | data formatting | bytes 6291456

commit v4 on v3

--- a/solution.py
+++ b/solution.py
@@ -34,34 +34,34 @@
 B_0 = (2 * HALF_A, HALF_B)
 B_1 = (2 * HALF_A + HALF_B, HALF_B)
 ORDER = (
-    ("A2", 0, 0), ("A1", 0), ("B1R", 0), ("B1L", 0), ("B3", 0, 0), ("A3R", 0, 0, 0), ("A3L", 0, 0, 0),
-    ("B4", 0, 0, 0), ("H", 0), ("T1",), ("H", 1), ("H", 2), ("H", 3), ("H", 4), ("H", 5), ("H", 6), ("H", 7),
-    ("B3", 0, -1), ("B3", 0, 1), ("B2R", 0), ("B2L", 0), ("B4", 0, -1, 0), ("B4", 0, 0, 1), ("A3R", 0, 1, 0),
-    ("A2", 0, 1), ("T2",), ("A3L", 0, 0, 1), ("A3R", 0, 0, 1), ("A3L", 0, 1, 0), ("B3", 0, 2), ("A2", 1, 0),
-    ("A1", 1), ("B4", 0, 1, 0), ("B1R", 1), ("B1L", 1), ("A4R", 0, 0, 0), ("A4L", 0, 0, 0), ("B3", 1, 0),
-    ("A4R", 0, 0, 1), ("A4L", 0, 0, 1), ("A4R", 0, 1, 0), ("A4L", 0, 1, 0), ("B3", 1, -1), ("B4", 0, -1, 1),
-    ("B2R", 1), ("B2L", 1), ("A3R", 0, 1, 1), ("A3L", 0, 1, 1), ("B3", 1, 1), ("B4", 0, 1, 1), ("A3R", 1, 0, 0),
-    ("A3L", 1, 0, 0), ("C", 0, 0, 0), ("T3",), ("A2", 1, 1), ("C", 0, 0, 1), ("B3", 1, 2), ("C", 0, 0, 2), ("A1", 2),
-    ("C", 0, 0, 3), ("A2", 2, 0), ("B1R", 2), ("B1L", 2), ("B4", 0, 2, 0), ("A4R", 0, 1, 1), ("A4L", 0, 1, 1),
-    ("A3R", 1, 0, 1), ("B3", 2, 0), ("A3L", 1, 0, 1), ("A3R", 1, 1, 0), ("A3L", 1, 1, 0), ("B3", 2, -1),
-    ("B4", 0, 2, 1), ("B4", 1, 0, 0), ("A2", 2, 1), ("B2R", 2), ("B2L", 2), ("A3R", 1, 1, 1), ("B3", 2, 1),
-    ("A3L", 1, 1, 1), ("A4R", 1, 0, 0), ("A4L", 1, 0, 0), ("B4", 1, 0, 1), ("B4", 1, -1, 0), ("B3", 2, 2),
-    ("C", 0, 1, 0), ("B1R", 3), ("B1L", 3), ("C", 0, 1, 1), ("A4R", 1, 0, 1), ("A4L", 1, 0, 1), ("A2", 3, 0),
-    ("C", 0, 1, 2), ("A1", 3), ("C", 0, 1, 3), ("B3", 3, 0), ("B4", 1, -1, 1), ("A4R", 1, 1, 0), ("A4L", 1, 1, 0),
-    ("A4R", 1, 1, 1), ("A4L", 1, 1, 1), ("B3", 3, -1), ("B4", 1, 1, 0), ("B2R", 3), ("B2L", 3), ("A3R", 2, 0, 0),
-    ("B4", 1, 1, 1), ("A3L", 2, 0, 0), ("B3", 3, 1), ("C", 1, 0, 0), ("A3R", 2, 0, 1), ("A2", 3, 1),
-    ("A3L", 2, 0, 1), ("C", 1, 0, 1), ("B4", 1, 2, 0), ("C", 1, 0, 2), ("C", 1, 0, 3), ("B4", 1, 2, 1), ("B3", 3, 2),
-    ("A3R", 2, 1, 0), ("A3L", 2, 1, 0), ("B4", 2, 0, 0), ("B4", 2, 0, 1), ("A3R", 2, 1, 1), ("A3L", 2, 1, 1),
-    ("C", 1, 1, 0), ("A4R", 2, 0, 0), ("A4L", 2, 0, 0), ("B4", 2, -1, 0), ("C", 1, 1, 1), ("C", 1, 1, 2),
-    ("C", 1, 1, 3), ("B4", 2, -1, 1), ("A4R", 2, 0, 1), ("A4L", 2, 0, 1), ("A4R", 2, 1, 0), ("A4L", 2, 1, 0),
-    ("B4", 2, 1, 0), ("B4", 2, 1, 1), ("A4R", 2, 1, 1), ("A4L", 2, 1, 1), ("A3R", 3, 0, 0), ("A3L", 3, 0, 0),
-    ("C", 2, 0, 0), ("B4", 2, 2, 0), ("B4", 2, 2, 1), ("A3R", 3, 0, 1), ("A3L", 3, 0, 1), ("C", 2, 0, 1),
-    ("C", 2, 0, 2), ("C", 2, 0, 3), ("A3R", 3, 1, 0), ("A3L", 3, 1, 0), ("B4", 3, 0, 0), ("B4", 3, 0, 1),
-    ("C", 2, 1, 0), ("A3R", 3, 1, 1), ("A3L", 3, 1, 1), ("C", 2, 1, 1), ("C", 2, 1, 2), ("A4R", 3, 0, 0),
-    ("A4L", 3, 0, 0), ("B4", 3, -1, 0), ("B4", 3, -1, 1), ("C", 2, 1, 3), ("C", 3, 0, 0), ("A4R", 3, 0, 1),
-    ("A4L", 3, 0, 1), ("B4", 3, 1, 0), ("B4", 3, 1, 1), ("A4R", 3, 1, 0), ("A4L", 3, 1, 0), ("A4R", 3, 1, 1),
-    ("A4L", 3, 1, 1), ("B4", 3, 2, 0), ("B4", 3, 2, 1), ("C", 3, 0, 1), ("C", 3, 0, 2), ("C", 3, 0, 3),
-    ("C", 3, 0, 4), ("C", 3, 1, 0), ("C", 3, 1, 1), ("C", 3, 1, 2), ("C", 3, 1, 3), ("C", 3, 1, 4),
+    ("A1", 0), ("A2", 0, 0), ("B1R", 0), ("B1L", 0), ("B3", 0, 0), ("A3R", 0, 0, 0), ("A3L", 0, 0, 0),
+    ("B4", 0, 0, 0), ("H", 0), ("T1",), ("T2",), ("T3",), ("H", 1), ("H", 2), ("H", 3), ("H", 4), ("H", 5), ("H", 6),
+    ("H", 7), ("B3", 0, -1), ("B3", 0, 1), ("B2R", 0), ("B2L", 0), ("A3R", 0, 1, 0), ("A3L", 0, 1, 0),
+    ("A4R", 0, 0, 0), ("A4L", 0, 0, 0), ("B3", 0, 2), ("B4", 0, 0, 1), ("B4", 0, -1, 0), ("A2", 0, 1),
+    ("A3R", 0, 0, 1), ("A3L", 0, 0, 1), ("A4R", 0, 1, 0), ("A4L", 0, 1, 0), ("A3R", 0, 1, 1), ("A3L", 0, 1, 1),
+    ("A4R", 0, 0, 1), ("A4L", 0, 0, 1), ("B4", 0, -1, 1), ("C", 0, 0, 0), ("B4", 0, 1, 0), ("C", 0, 0, 1),
+    ("C", 0, 0, 2), ("C", 0, 0, 3), ("A4R", 0, 1, 1), ("A4L", 0, 1, 1), ("A2", 1, 0), ("B1R", 1), ("B1L", 1),
+    ("B3", 1, 0), ("A3R", 1, 0, 0), ("A2", 2, 0), ("A1", 1), ("B1L", 2), ("B1R", 2), ("A3L", 1, 0, 0), ("A1", 2),
+    ("B1L", 3), ("B1R", 3), ("B3", 2, 0), ("B4", 0, 1, 1), ("A3L", 2, 0, 0), ("B2R", 1), ("B4", 0, 2, 0),
+    ("A2", 1, 1), ("A3R", 1, 0, 1), ("B3", 1, -1), ("B2L", 1), ("B4", 0, 2, 1), ("A3R", 1, 1, 0), ("A1", 3),
+    ("A3L", 1, 0, 1), ("B2R", 2), ("B3", 1, 1), ("A3L", 1, 1, 0), ("B4", 1, 0, 0), ("A4R", 1, 0, 0), ("B3", 1, 2),
+    ("B2L", 2), ("C", 0, 1, 0), ("A2", 2, 1), ("B4", 1, 0, 1), ("C", 0, 1, 1), ("A3R", 2, 0, 0), ("C", 0, 1, 2),
+    ("B3", 2, -1), ("C", 0, 1, 3), ("A3L", 1, 1, 1), ("B4", 1, -1, 0), ("A3R", 1, 1, 1), ("A4R", 1, 0, 1),
+    ("A4L", 1, 0, 0), ("B4", 1, -1, 1), ("B3", 2, 1), ("A4L", 1, 0, 1), ("B4", 1, 1, 0), ("A4R", 1, 1, 0),
+    ("B3", 2, 2), ("A4L", 1, 1, 0), ("B4", 1, 1, 1), ("A2", 3, 0), ("A3L", 2, 0, 1), ("A3R", 2, 0, 1),
+    ("B4", 1, 2, 0), ("A2", 3, 1), ("A3L", 2, 1, 0), ("A3R", 2, 1, 0), ("A3R", 2, 1, 1), ("B4", 1, 2, 1),
+    ("A4L", 1, 1, 1), ("C", 1, 0, 0), ("B3", 3, 0), ("B4", 2, 0, 0), ("B4", 2, 0, 1), ("C", 1, 0, 1), ("C", 1, 0, 2),
+    ("C", 1, 0, 3), ("A3L", 2, 1, 1), ("B3", 3, -1), ("B2L", 3), ("A4R", 1, 1, 1), ("B3", 3, 1), ("B4", 2, -1, 0),
+    ("B4", 2, -1, 1), ("A4L", 2, 0, 0), ("B2R", 3), ("A4R", 2, 0, 0), ("A4L", 2, 0, 1), ("A4R", 2, 0, 1),
+    ("A4R", 2, 1, 0), ("B4", 2, 1, 0), ("B4", 2, 1, 1), ("A4L", 2, 1, 0), ("C", 1, 1, 0), ("B3", 3, 2),
+    ("A4R", 2, 1, 1), ("A3L", 3, 0, 0), ("A3L", 3, 0, 1), ("C", 1, 1, 1), ("C", 1, 1, 2), ("A3R", 3, 0, 0),
+    ("A3R", 3, 0, 1), ("C", 1, 1, 3), ("B4", 2, 2, 0), ("B4", 2, 2, 1), ("A4L", 2, 1, 1), ("C", 2, 0, 0),
+    ("A3R", 3, 1, 0), ("C", 2, 0, 1), ("C", 2, 0, 2), ("C", 2, 0, 3), ("B4", 3, 0, 0), ("B4", 3, 0, 1),
+    ("A3L", 3, 1, 0), ("C", 2, 1, 0), ("A3L", 3, 1, 1), ("A3R", 3, 1, 1), ("A4L", 3, 0, 0), ("B4", 3, -1, 0),
+    ("B4", 3, -1, 1), ("A4R", 3, 0, 0), ("A4R", 3, 0, 1), ("A4L", 3, 0, 1), ("B4", 3, 1, 0), ("B4", 3, 1, 1),
+    ("A4R", 3, 1, 0), ("A4L", 3, 1, 0), ("C", 3, 0, 0), ("A4L", 3, 1, 1), ("B4", 3, 2, 0), ("B4", 3, 2, 1),
+    ("A4R", 3, 1, 1), ("C", 3, 0, 1), ("C", 3, 1, 0), ("C", 3, 1, 1), ("C", 2, 1, 1), ("C", 2, 1, 2), ("C", 2, 1, 3),
+    ("C", 3, 0, 2), ("C", 3, 0, 3), ("C", 3, 0, 4), ("C", 3, 1, 2), ("C", 3, 1, 3), ("C", 3, 1, 4),
 )
 SPLIT = ((3, False), (3, True))
 Y_FIRST = ()

time: 111 us -> 111 us (level)
  no operation moved by 1% of the time
where the time goes in v4:
time: 111 us
  Pallas kernels  108 us (97%)
  local copies, waits for them, and re-layouts  3.07 us (3%)
    pallas_call x1, Pallas kernels, body(): pl.pallas_call(kernel, out_shape=(pltpu.VMEM((SLOTS, UNITS), BF16), pltpu...  108 us
    unnamed x2, local copies, waits for them, and re-layouts  3.07 us

profile of v4, /device:TPU:1, one launch (start us, length us, event | category | flops | bytes accessed | tf_op | source)
XLA Modules:
  0.0 111.3 jit_solution(12622546504062411023)
XLA Ops:
  0.6 107.6 %dispatch_and_products.1 = (bf16[2304,512]{1,0:T(8,128)(2,1)S(1)}, bf16[512,3072]{1,0:T(8,128)(2,1)S(1)}) custom-call(s32[2,128]{1,0:T(2,128)} %bitcast.19, s32[2,128]{1,0:T(2,128)} %bitcast.20, f32[2,128]{1,0:T(2,128)} %bitcast.21, bf16[128,3072]{1,0:T(8,128)(2,1)} %bitcast.18, bf16[2304,512]{1,0:T(8,128)(2,1)} %bitcast.17, bf16[512,3072]{1,0:T(8,128)(2,1)} %bitcast.16), custom_call_target="tpu_custom_call" | custom-call | flops 15000000512 | bytes 12000000 | tf_op jit(solution)/shard_map/dispatch_and_products/pallas_call | solution.py:406
  108.2 1.4 %copy.10 = bf16[1,2304,512]{2,1,0:T(8,128)(2,1)} copy(bf16[1,2304,512]{2,1,0:T(8,128)(2,1)S(1)} %bitcast.15) | data formatting | bytes 4718592
  109.6 1.7 %copy.11 = bf16[1,512,3072]{2,1,0:T(8,128)(2,1)} copy(bf16[1,512,3072]{2,1,0:T(8,128)(2,1)S(1)} %bitcast.14) | data formatting | bytes 6291456
